TPU v7x, 512 devices: a whole 4x8x8 slice. The times are simulated.
512 devices in a mesh: energy: 16 (over x, y_hi), width: 32 (over z, y_lo, core).
Axes of the slice: x: 4, y: 8 (y_hi: 4, y_lo: 2; y = y_hi * 2 + y_lo), z: 8, core: 2. Of those that a mesh axis runs over, the one named last changes fastest.
Arguments:
- inverse_blocks: bfloat16 [32, 8192, 256], P('energy', 'width')
- source: bfloat16 [32, 8192, 512], P('energy', 'width'), may hold values from -6 to 6
- left_coupling: bfloat16 [1024, 256], P('width'), may hold values from -0.875 to 0.875
- right_coupling: bfloat16 [1024, 256], P('width'), may hold values from -0.875 to 0.875
- energy_weights: float32 [32], P('energy'), may hold values from 0.25 to 2
- collector_low: int32 [32], P('width'), may hold values from 0 to 63
- collector_high: int32 [32], P('width'), may hold values from 193 to 256
Outputs:
- gradient: float32 [32, 256, 256], P('width', 'energy')
Inputs may be any that keep to these rules, and one draw needn't show every extreme that they name: collector_low < 64 and collector_high > 192 for every strip.
All inputs are finite; a program needn't handle non-finite values.
Results may differ from a plain program's by a relative error of at most 0.0033.
Values may be sent and summed in bfloat16 or wider, within the bound.
No kernel may reach another device: no remote copies, remote signals or barrier semaphores. Data moves between devices by JAX's collectives and lax.ppermute only.
A program may use at most 64 MiB of HBM per device.

v0:
```python
import jax
import jax.numpy as jnp
from jax import lax
from jax.sharding import PartitionSpec as P

SWEEPS = 10


def with_halo(block, sides, width):
    for axis, dim in sides:
        count = lax.axis_size(axis)
        forward = [(i, i + 1) for i in range(count - 1)]
        forward.append((count - 1, 0))
        backward = [(target, source) for source, target in forward]
        low = lax.ppermute(
            lax.slice_in_dim(block, block.shape[dim] - width, None, axis=dim), axis, forward
        )
        high = lax.ppermute(lax.slice_in_dim(block, 0, width, axis=dim), axis, backward)
        block = jnp.concatenate([low, block, high], axis=dim)
    return block


def couple_rows(left_coupling, right_coupling, tails, heads):
    first = jnp.einsum("ei,kem->kim", left_coupling, tails, preferred_element_type=jnp.float32)
    second = jnp.einsum("ei,kem->kim", right_coupling, heads, preferred_element_type=jnp.float32)
    return first + second


def body(
    inverse_blocks,
    source,
    left_coupling,
    right_coupling,
    energy_weights,
    collector_low,
    collector_high,
):
    edge = left_coupling.shape[0]
    block = inverse_blocks.shape[1]
    count = inverse_blocks.shape[0]
    modes = source.shape[2]
    psi = jnp.einsum(
        "kij,kjm->kim", inverse_blocks, source, preferred_element_type=jnp.float32
    ).astype(jnp.bfloat16)

    def forward_sweep(sweep, psi):
        padded = with_halo(psi, (("width", 1),), edge)
        tails = padded[:, :edge]
        heads = padded[:, padded.shape[1] - edge :]
        couple = couple_rows(left_coupling, right_coupling, tails, heads)
        rhs = (source.astype(jnp.float32) + couple).astype(jnp.bfloat16)
        return jnp.einsum(
            "kij,kjm->kim", inverse_blocks, rhs, preferred_element_type=jnp.float32
        ).astype(jnp.bfloat16)

    psi = lax.fori_loop(0, SWEEPS - 1, forward_sweep, psi)
    rows = lax.iota(jnp.int32, block)
    mask = ((rows >= collector_low[0]) & (rows < collector_high[0])).astype(jnp.float32)
    adjoint_source = (
        2.0 * energy_weights[:, None, None] * mask[None, :, None] * psi.astype(jnp.float32)
    )
    lam = jnp.einsum(
        "kji,kjm->kim",
        inverse_blocks,
        adjoint_source.astype(jnp.bfloat16),
        preferred_element_type=jnp.float32,
    ).astype(jnp.bfloat16)
    middle = jnp.zeros((count, block - 2 * edge, modes), jnp.float32)

    def adjoint_sweep(sweep, lam):
        to_prev = jnp.einsum(
            "ei,kim->kem", left_coupling, lam, preferred_element_type=jnp.float32
        ).astype(jnp.bfloat16)
        to_next = jnp.einsum(
            "ei,kim->kem", right_coupling, lam, preferred_element_type=jnp.float32
        ).astype(jnp.bfloat16)
        outgoing = jnp.concatenate([to_prev, to_next], axis=1)
        padded = with_halo(outgoing, (("width", 1),), edge)
        from_prev = padded[:, :edge]
        from_next = padded[:, padded.shape[1] - edge :]
        extra = jnp.concatenate(
            [from_prev.astype(jnp.float32), middle, from_next.astype(jnp.float32)], axis=1
        )
        update = (adjoint_source + extra).astype(jnp.bfloat16)
        return jnp.einsum(
            "kji,kjm->kim", inverse_blocks, update, preferred_element_type=jnp.float32
        ).astype(jnp.bfloat16)

    lam = lax.fori_loop(0, SWEEPS - 1, adjoint_sweep, lam)
    owned = block // lax.axis_size("energy")
    product = jnp.einsum("kim,kjm->ij", lam, psi, preferred_element_type=jnp.float32)
    full = lax.psum(product * (-1.0 / modes), "energy")
    mine = lax.dynamic_slice_in_dim(full, lax.axis_index("energy") * owned, owned, 0)
    return mine.reshape(1, owned, block)


def solution(mesh):
    placed = (
        P("energy", "width", None),
        P("energy", "width", None),
        P("width", None),
        P("width", None),
        P("energy"),
        P("width"),
        P("width"),
    )
    return jax.shard_map(
        body, mesh=mesh, in_specs=placed, out_specs=P("width", "energy", None), check_vma=False
    )
```

profile of v0, /device:TPU:64, one launch (start us, length us, event | category | flops | bytes accessed | tf_op | source)
XLA Modules:
  0.0 456.8 jit_solution(2762212867480273165)
XLA Ops:
  9.8 123.9 %while.20 = (s32[]{:T(128)}, bf16[2,256,512]{1,2,0:T(8,128)(2,1)S(1)}, bf16[2,256,512]{1,2,0:T(8,128)(2,1)S(1)}, bf16[32,256]{1,0:T(8,128)(2,1)S(1)}, bf16[32,25...) while((s32[]{:T(128)}, bf16[2,256,512]{1,2,0:T(8,128)(2,1)S(1)}, ...), condition=%wide.region_1.0_spmd, body=%wide.region_0.0_spmd.sunk | while | flops 169082880 | bytes 4358301 | solution.py:56
  10.0 2.0 collective-permute-start
  12.0 2.3 collective-permute-start.1
  16.2 4.5 collective-permute-done.1
  21.3 1.9 collective-permute-start
  23.2 2.4 collective-permute-start.1
  25.6 2.3 collective-permute-done
  28.2 7.1 %collective-permute-done.1 = bf16[2,32,512]{1,2,0:T(8,128)(2,1)S(1)} collective-permute-done((bf16[2,32,512]{1,2,0:T(8,128)(2,1)S(1)}, bf16[2,32,512]{1,2,0:T(8,128)(2,1)S(1)}, u32[]{:S(2)}, u32[]{:S(2)}) %collective-permute-start.1) | collective-permute-done | bytes 65568 | tf_op jit(solution)/shard_map/while/body/eval_jaxpr/ppermute | solution.py:15
  36.0 1.9 collective-permute-start
  37.9 2.4 collective-permute-start.1
  40.3 2.5 collective-permute-done
  43.1 8.8 %collective-permute-done.1 = bf16[2,32,512]{1,2,0:T(8,128)(2,1)S(1)} collective-permute-done((bf16[2,32,512]{1,2,0:T(8,128)(2,1)S(1)}, bf16[2,32,512]{1,2,0:T(8,128)(2,1)S(1)}, u32[]{:S(2)}, u32[]{:S(2)}) %collective-permute-start.1) | collective-permute-done | bytes 65568 | tf_op jit(solution)/shard_map/while/body/eval_jaxpr/ppermute | solution.py:15
  52.5 1.9 collective-permute-start
  54.4 2.4 collective-permute-start.1
  56.9 2.5 collective-permute-done
  59.6 4.7 %collective-permute-done.1 = bf16[2,32,512]{1,2,0:T(8,128)(2,1)S(1)} collective-permute-done((bf16[2,32,512]{1,2,0:T(8,128)(2,1)S(1)}, bf16[2,32,512]{1,2,0:T(8,128)(2,1)S(1)}, u32[]{:S(2)}, u32[]{:S(2)}) %collective-permute-start.1) | collective-permute-done | bytes 65568 | tf_op jit(solution)/shard_map/while/body/eval_jaxpr/ppermute | solution.py:15
  64.9 1.9 collective-permute-start
  66.9 2.4 collective-permute-start.1
  69.3 2.5 collective-permute-done
  72.0 4.7 %collective-permute-done.1 = bf16[2,32,512]{1,2,0:T(8,128)(2,1)S(1)} collective-permute-done((bf16[2,32,512]{1,2,0:T(8,128)(2,1)S(1)}, bf16[2,32,512]{1,2,0:T(8,128)(2,1)S(1)}, u32[]{:S(2)}, u32[]{:S(2)}) %collective-permute-start.1) | collective-permute-done | bytes 65568 | tf_op jit(solution)/shard_map/while/body/eval_jaxpr/ppermute | solution.py:15
  77.4 1.9 collective-permute-start
  79.3 2.4 collective-permute-start.1
  81.7 2.5 collective-permute-done
  84.4 4.7 %collective-permute-done.1 = bf16[2,32,512]{1,2,0:T(8,128)(2,1)S(1)} collective-permute-done((bf16[2,32,512]{1,2,0:T(8,128)(2,1)S(1)}, bf16[2,32,512]{1,2,0:T(8,128)(2,1)S(1)}, u32[]{:S(2)}, u32[]{:S(2)}) %collective-permute-start.1) | collective-permute-done | bytes 65568 | tf_op jit(solution)/shard_map/while/body/eval_jaxpr/ppermute | solution.py:15
  89.9 1.9 collective-permute-start
  91.8 2.4 collective-permute-start.1
  94.2 2.5 collective-permute-done
  96.9 6.0 %collective-permute-done.1 = bf16[2,32,512]{1,2,0:T(8,128)(2,1)S(1)} collective-permute-done((bf16[2,32,512]{1,2,0:T(8,128)(2,1)S(1)}, bf16[2,32,512]{1,2,0:T(8,128)(2,1)S(1)}, u32[]{:S(2)}, u32[]{:S(2)}) %collective-permute-start.1) | collective-permute-done | bytes 65568 | tf_op jit(solution)/shard_map/while/body/eval_jaxpr/ppermute | solution.py:15
  103.7 1.9 collective-permute-start
  105.6 2.4 collective-permute-start.1
  108.0 2.5 collective-permute-done
  110.7 7.3 %collective-permute-done.1 = bf16[2,32,512]{1,2,0:T(8,128)(2,1)S(1)} collective-permute-done((bf16[2,32,512]{1,2,0:T(8,128)(2,1)S(1)}, bf16[2,32,512]{1,2,0:T(8,128)(2,1)S(1)}, u32[]{:S(2)}, u32[]{:S(2)}) %collective-permute-start.1) | collective-permute-done | bytes 65568 | tf_op jit(solution)/shard_map/while/body/eval_jaxpr/ppermute | solution.py:15
  118.8 1.9 collective-permute-start
  120.7 2.4 collective-permute-start.1
  123.1 2.5 collective-permute-done
  125.8 7.4 %collective-permute-done.1 = bf16[2,32,512]{1,2,0:T(8,128)(2,1)S(1)} collective-permute-done((bf16[2,32,512]{1,2,0:T(8,128)(2,1)S(1)}, bf16[2,32,512]{1,2,0:T(8,128)(2,1)S(1)}, u32[]{:S(2)}, u32[]{:S(2)}) %collective-permute-start.1) | collective-permute-done | bytes 65568 | tf_op jit(solution)/shard_map/while/body/eval_jaxpr/ppermute | solution.py:15
  134.1 137.8 %while.21 = (s32[]{:T(128)}, bf16[2,256,512]{1,2,0:T(8,128)(2,1)S(1)}, bf16[32,256]{1,0:T(8,128)(2,1)S(1)}, bf16[32,256]{1,0:T(8,128)(2,1)S(1)}, f32[2,256,512]{...) while((s32[]{:T(128)}, bf16[2,256,512]{1,2,0:T(8,128)(2,1)S(1)}, ...), condition=%wide.region_3.0_spmd, body=%wide.region_2.0_spmd.sunk | while | flops 169213952 | bytes 4230837 | solution.py:89
  134.4 1.9 collective-permute-start.2
  136.6 2.4 collective-permute-start.3
  141.0 7.9 %collective-permute-done.3 = bf16[2,32,512]{1,2,0:T(8,128)(2,1)S(1)} collective-permute-done((bf16[2,32,512]{1,2,0:T(8,128)(2,1)S(1)}, bf16[2,32,512]{1,2,0:T(8,128)(2,1)S(1)}, u32[]{:S(2)}, u32[]{:S(2)}) %collective-permute-start.3) | collective-permute-done | bytes 65568 | tf_op jit(solution)/shard_map/while/body/eval_jaxpr/ppermute | solution.py:15
  149.6 1.9 collective-permute-start.2
  151.8 2.4 collective-permute-start.3
  156.1 7.6 %collective-permute-done.3 = bf16[2,32,512]{1,2,0:T(8,128)(2,1)S(1)} collective-permute-done((bf16[2,32,512]{1,2,0:T(8,128)(2,1)S(1)}, bf16[2,32,512]{1,2,0:T(8,128)(2,1)S(1)}, u32[]{:S(2)}, u32[]{:S(2)}) %collective-permute-start.3) | collective-permute-done | bytes 65568 | tf_op jit(solution)/shard_map/while/body/eval_jaxpr/ppermute | solution.py:15
  164.4 1.9 collective-permute-start.2
  166.6 2.4 collective-permute-start.3
  171.0 8.1 %collective-permute-done.3 = bf16[2,32,512]{1,2,0:T(8,128)(2,1)S(1)} collective-permute-done((bf16[2,32,512]{1,2,0:T(8,128)(2,1)S(1)}, bf16[2,32,512]{1,2,0:T(8,128)(2,1)S(1)}, u32[]{:S(2)}, u32[]{:S(2)}) %collective-permute-start.3) | collective-permute-done | bytes 65568 | tf_op jit(solution)/shard_map/while/body/eval_jaxpr/ppermute | solution.py:15
  179.8 1.9 collective-permute-start.2
  182.0 2.4 collective-permute-start.3
  186.3 8.1 %collective-permute-done.3 = bf16[2,32,512]{1,2,0:T(8,128)(2,1)S(1)} collective-permute-done((bf16[2,32,512]{1,2,0:T(8,128)(2,1)S(1)}, bf16[2,32,512]{1,2,0:T(8,128)(2,1)S(1)}, u32[]{:S(2)}, u32[]{:S(2)}) %collective-permute-start.3) | collective-permute-done | bytes 65568 | tf_op jit(solution)/shard_map/while/body/eval_jaxpr/ppermute | solution.py:15
  195.1 1.9 collective-permute-start.2
  197.3 2.4 collective-permute-start.3
  201.7 8.2 %collective-permute-done.3 = bf16[2,32,512]{1,2,0:T(8,128)(2,1)S(1)} collective-permute-done((bf16[2,32,512]{1,2,0:T(8,128)(2,1)S(1)}, bf16[2,32,512]{1,2,0:T(8,128)(2,1)S(1)}, u32[]{:S(2)}, u32[]{:S(2)}) %collective-permute-start.3) | collective-permute-done | bytes 65568 | tf_op jit(solution)/shard_map/while/body/eval_jaxpr/ppermute | solution.py:15
  210.6 1.9 collective-permute-start.2
  212.8 2.4 collective-permute-start.3
  217.1 8.2 %collective-permute-done.3 = bf16[2,32,512]{1,2,0:T(8,128)(2,1)S(1)} collective-permute-done((bf16[2,32,512]{1,2,0:T(8,128)(2,1)S(1)}, bf16[2,32,512]{1,2,0:T(8,128)(2,1)S(1)}, u32[]{:S(2)}, u32[]{:S(2)}) %collective-permute-start.3) | collective-permute-done | bytes 65568 | tf_op jit(solution)/shard_map/while/body/eval_jaxpr/ppermute | solution.py:15
  226.0 1.9 collective-permute-start.2
  228.2 2.4 collective-permute-start.3
  232.5 8.2 %collective-permute-done.3 = bf16[2,32,512]{1,2,0:T(8,128)(2,1)S(1)} collective-permute-done((bf16[2,32,512]{1,2,0:T(8,128)(2,1)S(1)}, bf16[2,32,512]{1,2,0:T(8,128)(2,1)S(1)}, u32[]{:S(2)}, u32[]{:S(2)}) %collective-permute-start.3) | collective-permute-done | bytes 65568 | tf_op jit(solution)/shard_map/while/body/eval_jaxpr/ppermute | solution.py:15
  241.4 1.9 collective-permute-start.2
  243.6 2.4 collective-permute-start.3
  248.0 8.2 %collective-permute-done.3 = bf16[2,32,512]{1,2,0:T(8,128)(2,1)S(1)} collective-permute-done((bf16[2,32,512]{1,2,0:T(8,128)(2,1)S(1)}, bf16[2,32,512]{1,2,0:T(8,128)(2,1)S(1)}, u32[]{:S(2)}, u32[]{:S(2)}) %collective-permute-start.3) | collective-permute-done | bytes 65568 | tf_op jit(solution)/shard_map/while/body/eval_jaxpr/ppermute | solution.py:15
  259.0 2.4 collective-permute-start.3
  263.4 8.2 %collective-permute-done.3 = bf16[2,32,512]{1,2,0:T(8,128)(2,1)S(1)} collective-permute-done((bf16[2,32,512]{1,2,0:T(8,128)(2,1)S(1)}, bf16[2,32,512]{1,2,0:T(8,128)(2,1)S(1)}, u32[]{:S(2)}, u32[]{:S(2)}) %collective-permute-start.3) | collective-permute-done | bytes 65568 | tf_op jit(solution)/shard_map/while/body/eval_jaxpr/ppermute | solution.py:15
  273.0 175.6 %all-reduce.2.cloned.1.call-done = f32[256,256]{1,0:T(8,128)} async-done(((f32[256,256]{1,0:T(8,128)}), f32[256,256]{1,0:T(8,128)}) %all-reduce.2.cloned.1.call-update) | async-done | bytes 262160 | tf_op jit(solution)/shard_map/psum | solution.py:92
  (123 shorter events, 42.2 us)
Async XLA Ops:
  6.5 1.3 copy-start.1
  6.5 1.3 copy-start
  6.5 442.1 %all-reduce.2.cloned.1.call-start = ((), (), s32[]{:S(2)}) async-start(), calls=%async_computation | async-start | bytes 524288 | tf_op jit(solution)/shard_map/psum | solution.py:92
  8.2 1.6 copy-start.4
  8.2 1.6 copy-start.3
  8.4 1.4 copy-start.2
  10.0 5.9 %collective-permute-start = (bf16[2,32,512]{1,2,0:T(8,128)(2,1)S(1)}, bf16[2,32,512]{1,2,0:T(8,128)(2,1)S(1)}, u32[]{:S(2)}, u32[]{:S(2)}) collective-permute-start(bf16[2,32,512]{1,2,0:T(8,128)(2,1)S(1)} %get-tuple-element.173), channel_id=1, source_target_pairs={{1,0},{2,1},{3,2},{4,3},{5,4},{6,5},{7,6},{8,7},{9,8},{10,9},{11,1... | collective-permute-start | bytes 196616 | tf_op jit(solution)/shard_map/while/body/eval_jaxpr/ppermute | solution.py:18
  12.0 8.6 %collective-permute-start.1 = (bf16[2,32,512]{1,2,0:T(8,128)(2,1)S(1)}, bf16[2,32,512]{1,2,0:T(8,128)(2,1)S(1)}, u32[]{:S(2)}, u32[]{:S(2)}) collective-permute-start(bf16[2,32,512]{1,2,0:T(8,128)(2,1)S(1)} %get-tuple-element.174), channel_id=1, source_target_pairs={{0,1},{1,2},{2,3},{3,4},{4,5},{5,6},{6,7},{7,8},{8,9},{9,10},{10,1... | collective-permute-start | bytes 196616 | tf_op jit(solution)/shard_map/while/body/eval_jaxpr/ppermute | solution.py:15
  21.3 6.6 %collective-permute-start = (bf16[2,32,512]{1,2,0:T(8,128)(2,1)S(1)}, bf16[2,32,512]{1,2,0:T(8,128)(2,1)S(1)}, u32[]{:S(2)}, u32[]{:S(2)}) collective-permute-start(bf16[2,32,512]{1,2,0:T(8,128)(2,1)S(1)} %get-tuple-element.173), channel_id=1, source_target_pairs={{1,0},{2,1},{3,2},{4,3},{5,4},{6,5},{7,6},{8,7},{9,8},{10,9},{11,1... | collective-permute-start | bytes 196616 | tf_op jit(solution)/shard_map/while/body/eval_jaxpr/ppermute | solution.py:18
  23.2 12.1 %collective-permute-start.1 = (bf16[2,32,512]{1,2,0:T(8,128)(2,1)S(1)}, bf16[2,32,512]{1,2,0:T(8,128)(2,1)S(1)}, u32[]{:S(2)}, u32[]{:S(2)}) collective-permute-start(bf16[2,32,512]{1,2,0:T(8,128)(2,1)S(1)} %get-tuple-element.174), channel_id=1, source_target_pairs={{0,1},{1,2},{2,3},{3,4},{4,5},{5,6},{6,7},{7,8},{8,9},{9,10},{10,1... | collective-permute-start | bytes 196616 | tf_op jit(solution)/shard_map/while/body/eval_jaxpr/ppermute | solution.py:15
  36.0 6.8 %collective-permute-start = (bf16[2,32,512]{1,2,0:T(8,128)(2,1)S(1)}, bf16[2,32,512]{1,2,0:T(8,128)(2,1)S(1)}, u32[]{:S(2)}, u32[]{:S(2)}) collective-permute-start(bf16[2,32,512]{1,2,0:T(8,128)(2,1)S(1)} %get-tuple-element.173), channel_id=1, source_target_pairs={{1,0},{2,1},{3,2},{4,3},{5,4},{6,5},{7,6},{8,7},{9,8},{10,9},{11,1... | collective-permute-start | bytes 196616 | tf_op jit(solution)/shard_map/while/body/eval_jaxpr/ppermute | solution.py:18
  37.9 13.9 %collective-permute-start.1 = (bf16[2,32,512]{1,2,0:T(8,128)(2,1)S(1)}, bf16[2,32,512]{1,2,0:T(8,128)(2,1)S(1)}, u32[]{:S(2)}, u32[]{:S(2)}) collective-permute-start(bf16[2,32,512]{1,2,0:T(8,128)(2,1)S(1)} %get-tuple-element.174), channel_id=1, source_target_pairs={{0,1},{1,2},{2,3},{3,4},{4,5},{5,6},{6,7},{7,8},{8,9},{9,10},{10,1... | collective-permute-start | bytes 196616 | tf_op jit(solution)/shard_map/while/body/eval_jaxpr/ppermute | solution.py:15
  52.5 6.8 %collective-permute-start = (bf16[2,32,512]{1,2,0:T(8,128)(2,1)S(1)}, bf16[2,32,512]{1,2,0:T(8,128)(2,1)S(1)}, u32[]{:S(2)}, u32[]{:S(2)}) collective-permute-start(bf16[2,32,512]{1,2,0:T(8,128)(2,1)S(1)} %get-tuple-element.173), channel_id=1, source_target_pairs={{1,0},{2,1},{3,2},{4,3},{5,4},{6,5},{7,6},{8,7},{9,8},{10,9},{11,1... | collective-permute-start | bytes 196616 | tf_op jit(solution)/shard_map/while/body/eval_jaxpr/ppermute | solution.py:18
  54.4 9.8 %collective-permute-start.1 = (bf16[2,32,512]{1,2,0:T(8,128)(2,1)S(1)}, bf16[2,32,512]{1,2,0:T(8,128)(2,1)S(1)}, u32[]{:S(2)}, u32[]{:S(2)}) collective-permute-start(bf16[2,32,512]{1,2,0:T(8,128)(2,1)S(1)} %get-tuple-element.174), channel_id=1, source_target_pairs={{0,1},{1,2},{2,3},{3,4},{4,5},{5,6},{6,7},{7,8},{8,9},{9,10},{10,1... | collective-permute-start | bytes 196616 | tf_op jit(solution)/shard_map/while/body/eval_jaxpr/ppermute | solution.py:15
  64.9 6.8 %collective-permute-start = (bf16[2,32,512]{1,2,0:T(8,128)(2,1)S(1)}, bf16[2,32,512]{1,2,0:T(8,128)(2,1)S(1)}, u32[]{:S(2)}, u32[]{:S(2)}) collective-permute-start(bf16[2,32,512]{1,2,0:T(8,128)(2,1)S(1)} %get-tuple-element.173), channel_id=1, source_target_pairs={{1,0},{2,1},{3,2},{4,3},{5,4},{6,5},{7,6},{8,7},{9,8},{10,9},{11,1... | collective-permute-start | bytes 196616 | tf_op jit(solution)/shard_map/while/body/eval_jaxpr/ppermute | solution.py:18
  66.9 9.8 %collective-permute-start.1 = (bf16[2,32,512]{1,2,0:T(8,128)(2,1)S(1)}, bf16[2,32,512]{1,2,0:T(8,128)(2,1)S(1)}, u32[]{:S(2)}, u32[]{:S(2)}) collective-permute-start(bf16[2,32,512]{1,2,0:T(8,128)(2,1)S(1)} %get-tuple-element.174), channel_id=1, source_target_pairs={{0,1},{1,2},{2,3},{3,4},{4,5},{5,6},{6,7},{7,8},{8,9},{9,10},{10,1... | collective-permute-start | bytes 196616 | tf_op jit(solution)/shard_map/while/body/eval_jaxpr/ppermute | solution.py:15
  77.4 6.8 %collective-permute-start = (bf16[2,32,512]{1,2,0:T(8,128)(2,1)S(1)}, bf16[2,32,512]{1,2,0:T(8,128)(2,1)S(1)}, u32[]{:S(2)}, u32[]{:S(2)}) collective-permute-start(bf16[2,32,512]{1,2,0:T(8,128)(2,1)S(1)} %get-tuple-element.173), channel_id=1, source_target_pairs={{1,0},{2,1},{3,2},{4,3},{5,4},{6,5},{7,6},{8,7},{9,8},{10,9},{11,1... | collective-permute-start | bytes 196616 | tf_op jit(solution)/shard_map/while/body/eval_jaxpr/ppermute | solution.py:18
  79.3 9.9 %collective-permute-start.1 = (bf16[2,32,512]{1,2,0:T(8,128)(2,1)S(1)}, bf16[2,32,512]{1,2,0:T(8,128)(2,1)S(1)}, u32[]{:S(2)}, u32[]{:S(2)}) collective-permute-start(bf16[2,32,512]{1,2,0:T(8,128)(2,1)S(1)} %get-tuple-element.174), channel_id=1, source_target_pairs={{0,1},{1,2},{2,3},{3,4},{4,5},{5,6},{6,7},{7,8},{8,9},{9,10},{10,1... | collective-permute-start | bytes 196616 | tf_op jit(solution)/shard_map/while/body/eval_jaxpr/ppermute | solution.py:15
  89.9 6.8 %collective-permute-start = (bf16[2,32,512]{1,2,0:T(8,128)(2,1)S(1)}, bf16[2,32,512]{1,2,0:T(8,128)(2,1)S(1)}, u32[]{:S(2)}, u32[]{:S(2)}) collective-permute-start(bf16[2,32,512]{1,2,0:T(8,128)(2,1)S(1)} %get-tuple-element.173), channel_id=1, source_target_pairs={{1,0},{2,1},{3,2},{4,3},{5,4},{6,5},{7,6},{8,7},{9,8},{10,9},{11,1... | collective-permute-start | bytes 196616 | tf_op jit(solution)/shard_map/while/body/eval_jaxpr/ppermute | solution.py:18
  91.8 11.2 %collective-permute-start.1 = (bf16[2,32,512]{1,2,0:T(8,128)(2,1)S(1)}, bf16[2,32,512]{1,2,0:T(8,128)(2,1)S(1)}, u32[]{:S(2)}, u32[]{:S(2)}) collective-permute-start(bf16[2,32,512]{1,2,0:T(8,128)(2,1)S(1)} %get-tuple-element.174), channel_id=1, source_target_pairs={{0,1},{1,2},{2,3},{3,4},{4,5},{5,6},{6,7},{7,8},{8,9},{9,10},{10,1... | collective-permute-start | bytes 196616 | tf_op jit(solution)/shard_map/while/body/eval_jaxpr/ppermute | solution.py:15
  103.7 6.8 %collective-permute-start = (bf16[2,32,512]{1,2,0:T(8,128)(2,1)S(1)}, bf16[2,32,512]{1,2,0:T(8,128)(2,1)S(1)}, u32[]{:S(2)}, u32[]{:S(2)}) collective-permute-start(bf16[2,32,512]{1,2,0:T(8,128)(2,1)S(1)} %get-tuple-element.173), channel_id=1, source_target_pairs={{1,0},{2,1},{3,2},{4,3},{5,4},{6,5},{7,6},{8,7},{9,8},{10,9},{11,1... | collective-permute-start | bytes 196616 | tf_op jit(solution)/shard_map/while/body/eval_jaxpr/ppermute | solution.py:18
  105.6 12.5 %collective-permute-start.1 = (bf16[2,32,512]{1,2,0:T(8,128)(2,1)S(1)}, bf16[2,32,512]{1,2,0:T(8,128)(2,1)S(1)}, u32[]{:S(2)}, u32[]{:S(2)}) collective-permute-start(bf16[2,32,512]{1,2,0:T(8,128)(2,1)S(1)} %get-tuple-element.174), channel_id=1, source_target_pairs={{0,1},{1,2},{2,3},{3,4},{4,5},{5,6},{6,7},{7,8},{8,9},{9,10},{10,1... | collective-permute-start | bytes 196616 | tf_op jit(solution)/shard_map/while/body/eval_jaxpr/ppermute | solution.py:15
  118.8 6.8 %collective-permute-start = (bf16[2,32,512]{1,2,0:T(8,128)(2,1)S(1)}, bf16[2,32,512]{1,2,0:T(8,128)(2,1)S(1)}, u32[]{:S(2)}, u32[]{:S(2)}) collective-permute-start(bf16[2,32,512]{1,2,0:T(8,128)(2,1)S(1)} %get-tuple-element.173), channel_id=1, source_target_pairs={{1,0},{2,1},{3,2},{4,3},{5,4},{6,5},{7,6},{8,7},{9,8},{10,9},{11,1... | collective-permute-start | bytes 196616 | tf_op jit(solution)/shard_map/while/body/eval_jaxpr/ppermute | solution.py:18
  120.7 12.5 %collective-permute-start.1 = (bf16[2,32,512]{1,2,0:T(8,128)(2,1)S(1)}, bf16[2,32,512]{1,2,0:T(8,128)(2,1)S(1)}, u32[]{:S(2)}, u32[]{:S(2)}) collective-permute-start(bf16[2,32,512]{1,2,0:T(8,128)(2,1)S(1)} %get-tuple-element.174), channel_id=1, source_target_pairs={{0,1},{1,2},{2,3},{3,4},{4,5},{5,6},{6,7},{7,8},{8,9},{9,10},{10,1... | collective-permute-start | bytes 196616 | tf_op jit(solution)/shard_map/while/body/eval_jaxpr/ppermute | solution.py:15
  134.4 6.5 %collective-permute-start.2 = (bf16[2,32,512]{1,2,0:T(8,128)(2,1)S(1)}, bf16[2,32,512]{1,2,0:T(8,128)(2,1)S(1)}, u32[]{:S(2)}, u32[]{:S(2)}) collective-permute-start(bf16[2,32,512]{1,2,0:T(8,128)(2,1)S(1)} %fusion.64), channel_id=1, source_target_pairs={{1,0},{2,1},{3,2},{4,3},{5,4},{6,5},{7,6},{8,7},{9,8},{10,9},{11,1... | collective-permute-start | bytes 196616 | tf_op jit(solution)/shard_map/while/body/eval_jaxpr/ppermute | solution.py:18
  136.6 12.3 %collective-permute-start.3 = (bf16[2,32,512]{1,2,0:T(8,128)(2,1)S(1)}, bf16[2,32,512]{1,2,0:T(8,128)(2,1)S(1)}, u32[]{:S(2)}, u32[]{:S(2)}) collective-permute-start(bf16[2,32,512]{1,2,0:T(8,128)(2,1)S(1)} %fusion.65), channel_id=1, source_target_pairs={{0,1},{1,2},{2,3},{3,4},{4,5},{5,6},{6,7},{7,8},{8,9},{9,10},{10,1... | collective-permute-start | bytes 196616 | tf_op jit(solution)/shard_map/while/body/eval_jaxpr/ppermute | solution.py:15
  149.6 6.5 %collective-permute-start.2 = (bf16[2,32,512]{1,2,0:T(8,128)(2,1)S(1)}, bf16[2,32,512]{1,2,0:T(8,128)(2,1)S(1)}, u32[]{:S(2)}, u32[]{:S(2)}) collective-permute-start(bf16[2,32,512]{1,2,0:T(8,128)(2,1)S(1)} %fusion.64), channel_id=1, source_target_pairs={{1,0},{2,1},{3,2},{4,3},{5,4},{6,5},{7,6},{8,7},{9,8},{10,9},{11,1... | collective-permute-start | bytes 196616 | tf_op jit(solution)/shard_map/while/body/eval_jaxpr/ppermute | solution.py:18
  151.8 12.0 %collective-permute-start.3 = (bf16[2,32,512]{1,2,0:T(8,128)(2,1)S(1)}, bf16[2,32,512]{1,2,0:T(8,128)(2,1)S(1)}, u32[]{:S(2)}, u32[]{:S(2)}) collective-permute-start(bf16[2,32,512]{1,2,0:T(8,128)(2,1)S(1)} %fusion.65), channel_id=1, source_target_pairs={{0,1},{1,2},{2,3},{3,4},{4,5},{5,6},{6,7},{7,8},{8,9},{9,10},{10,1... | collective-permute-start | bytes 196616 | tf_op jit(solution)/shard_map/while/body/eval_jaxpr/ppermute | solution.py:15
  164.4 6.5 %collective-permute-start.2 = (bf16[2,32,512]{1,2,0:T(8,128)(2,1)S(1)}, bf16[2,32,512]{1,2,0:T(8,128)(2,1)S(1)}, u32[]{:S(2)}, u32[]{:S(2)}) collective-permute-start(bf16[2,32,512]{1,2,0:T(8,128)(2,1)S(1)} %fusion.64), channel_id=1, source_target_pairs={{1,0},{2,1},{3,2},{4,3},{5,4},{6,5},{7,6},{8,7},{9,8},{10,9},{11,1... | collective-permute-start | bytes 196616 | tf_op jit(solution)/shard_map/while/body/eval_jaxpr/ppermute | solution.py:18
  166.6 12.4 %collective-permute-start.3 = (bf16[2,32,512]{1,2,0:T(8,128)(2,1)S(1)}, bf16[2,32,512]{1,2,0:T(8,128)(2,1)S(1)}, u32[]{:S(2)}, u32[]{:S(2)}) collective-permute-start(bf16[2,32,512]{1,2,0:T(8,128)(2,1)S(1)} %fusion.65), channel_id=1, source_target_pairs={{0,1},{1,2},{2,3},{3,4},{4,5},{5,6},{6,7},{7,8},{8,9},{9,10},{10,1... | collective-permute-start | bytes 196616 | tf_op jit(solution)/shard_map/while/body/eval_jaxpr/ppermute | solution.py:15
  179.8 6.5 %collective-permute-start.2 = (bf16[2,32,512]{1,2,0:T(8,128)(2,1)S(1)}, bf16[2,32,512]{1,2,0:T(8,128)(2,1)S(1)}, u32[]{:S(2)}, u32[]{:S(2)}) collective-permute-start(bf16[2,32,512]{1,2,0:T(8,128)(2,1)S(1)} %fusion.64), channel_id=1, source_target_pairs={{1,0},{2,1},{3,2},{4,3},{5,4},{6,5},{7,6},{8,7},{9,8},{10,9},{11,1... | collective-permute-start | bytes 196616 | tf_op jit(solution)/shard_map/while/body/eval_jaxpr/ppermute | solution.py:18
  182.0 12.5 %collective-permute-start.3 = (bf16[2,32,512]{1,2,0:T(8,128)(2,1)S(1)}, bf16[2,32,512]{1,2,0:T(8,128)(2,1)S(1)}, u32[]{:S(2)}, u32[]{:S(2)}) collective-permute-start(bf16[2,32,512]{1,2,0:T(8,128)(2,1)S(1)} %fusion.65), channel_id=1, source_target_pairs={{0,1},{1,2},{2,3},{3,4},{4,5},{5,6},{6,7},{7,8},{8,9},{9,10},{10,1... | collective-permute-start | bytes 196616 | tf_op jit(solution)/shard_map/while/body/eval_jaxpr/ppermute | solution.py:15
  195.1 6.5 %collective-permute-start.2 = (bf16[2,32,512]{1,2,0:T(8,128)(2,1)S(1)}, bf16[2,32,512]{1,2,0:T(8,128)(2,1)S(1)}, u32[]{:S(2)}, u32[]{:S(2)}) collective-permute-start(bf16[2,32,512]{1,2,0:T(8,128)(2,1)S(1)} %fusion.64), channel_id=1, source_target_pairs={{1,0},{2,1},{3,2},{4,3},{5,4},{6,5},{7,6},{8,7},{9,8},{10,9},{11,1... | collective-permute-start | bytes 196616 | tf_op jit(solution)/shard_map/while/body/eval_jaxpr/ppermute | solution.py:18
  197.3 12.5 %collective-permute-start.3 = (bf16[2,32,512]{1,2,0:T(8,128)(2,1)S(1)}, bf16[2,32,512]{1,2,0:T(8,128)(2,1)S(1)}, u32[]{:S(2)}, u32[]{:S(2)}) collective-permute-start(bf16[2,32,512]{1,2,0:T(8,128)(2,1)S(1)} %fusion.65), channel_id=1, source_target_pairs={{0,1},{1,2},{2,3},{3,4},{4,5},{5,6},{6,7},{7,8},{8,9},{9,10},{10,1... | collective-permute-start | bytes 196616 | tf_op jit(solution)/shard_map/while/body/eval_jaxpr/ppermute | solution.py:15
  210.6 6.5 %collective-permute-start.2 = (bf16[2,32,512]{1,2,0:T(8,128)(2,1)S(1)}, bf16[2,32,512]{1,2,0:T(8,128)(2,1)S(1)}, u32[]{:S(2)}, u32[]{:S(2)}) collective-permute-start(bf16[2,32,512]{1,2,0:T(8,128)(2,1)S(1)} %fusion.64), channel_id=1, source_target_pairs={{1,0},{2,1},{3,2},{4,3},{5,4},{6,5},{7,6},{8,7},{9,8},{10,9},{11,1... | collective-permute-start | bytes 196616 | tf_op jit(solution)/shard_map/while/body/eval_jaxpr/ppermute | solution.py:18
  212.8 12.5 %collective-permute-start.3 = (bf16[2,32,512]{1,2,0:T(8,128)(2,1)S(1)}, bf16[2,32,512]{1,2,0:T(8,128)(2,1)S(1)}, u32[]{:S(2)}, u32[]{:S(2)}) collective-permute-start(bf16[2,32,512]{1,2,0:T(8,128)(2,1)S(1)} %fusion.65), channel_id=1, source_target_pairs={{0,1},{1,2},{2,3},{3,4},{4,5},{5,6},{6,7},{7,8},{8,9},{9,10},{10,1... | collective-permute-start | bytes 196616 | tf_op jit(solution)/shard_map/while/body/eval_jaxpr/ppermute | solution.py:15
  226.0 6.5 %collective-permute-start.2 = (bf16[2,32,512]{1,2,0:T(8,128)(2,1)S(1)}, bf16[2,32,512]{1,2,0:T(8,128)(2,1)S(1)}, u32[]{:S(2)}, u32[]{:S(2)}) collective-permute-start(bf16[2,32,512]{1,2,0:T(8,128)(2,1)S(1)} %fusion.64), channel_id=1, source_target_pairs={{1,0},{2,1},{3,2},{4,3},{5,4},{6,5},{7,6},{8,7},{9,8},{10,9},{11,1... | collective-permute-start | bytes 196616 | tf_op jit(solution)/shard_map/while/body/eval_jaxpr/ppermute | solution.py:18
  228.2 12.5 %collective-permute-start.3 = (bf16[2,32,512]{1,2,0:T(8,128)(2,1)S(1)}, bf16[2,32,512]{1,2,0:T(8,128)(2,1)S(1)}, u32[]{:S(2)}, u32[]{:S(2)}) collective-permute-start(bf16[2,32,512]{1,2,0:T(8,128)(2,1)S(1)} %fusion.65), channel_id=1, source_target_pairs={{0,1},{1,2},{2,3},{3,4},{4,5},{5,6},{6,7},{7,8},{8,9},{9,10},{10,1... | collective-permute-start | bytes 196616 | tf_op jit(solution)/shard_map/while/body/eval_jaxpr/ppermute | solution.py:15
  241.4 6.5 %collective-permute-start.2 = (bf16[2,32,512]{1,2,0:T(8,128)(2,1)S(1)}, bf16[2,32,512]{1,2,0:T(8,128)(2,1)S(1)}, u32[]{:S(2)}, u32[]{:S(2)}) collective-permute-start(bf16[2,32,512]{1,2,0:T(8,128)(2,1)S(1)} %fusion.64), channel_id=1, source_target_pairs={{1,0},{2,1},{3,2},{4,3},{5,4},{6,5},{7,6},{8,7},{9,8},{10,9},{11,1... | collective-permute-start | bytes 196616 | tf_op jit(solution)/shard_map/while/body/eval_jaxpr/ppermute | solution.py:18
  243.6 12.5 %collective-permute-start.3 = (bf16[2,32,512]{1,2,0:T(8,128)(2,1)S(1)}, bf16[2,32,512]{1,2,0:T(8,128)(2,1)S(1)}, u32[]{:S(2)}, u32[]{:S(2)}) collective-permute-start(bf16[2,32,512]{1,2,0:T(8,128)(2,1)S(1)} %fusion.65), channel_id=1, source_target_pairs={{0,1},{1,2},{2,3},{3,4},{4,5},{5,6},{6,7},{7,8},{8,9},{9,10},{10,1... | collective-permute-start | bytes 196616 | tf_op jit(solution)/shard_map/while/body/eval_jaxpr/ppermute | solution.py:15
  256.8 6.5 %collective-permute-start.2 = (bf16[2,32,512]{1,2,0:T(8,128)(2,1)S(1)}, bf16[2,32,512]{1,2,0:T(8,128)(2,1)S(1)}, u32[]{:S(2)}, u32[]{:S(2)}) collective-permute-start(bf16[2,32,512]{1,2,0:T(8,128)(2,1)S(1)} %fusion.64), channel_id=1, source_target_pairs={{1,0},{2,1},{3,2},{4,3},{5,4},{6,5},{7,6},{8,7},{9,8},{10,9},{11,1... | collective-permute-start | bytes 196616 | tf_op jit(solution)/shard_map/while/body/eval_jaxpr/ppermute | solution.py:18
  259.0 12.5 %collective-permute-start.3 = (bf16[2,32,512]{1,2,0:T(8,128)(2,1)S(1)}, bf16[2,32,512]{1,2,0:T(8,128)(2,1)S(1)}, u32[]{:S(2)}, u32[]{:S(2)}) collective-permute-start(bf16[2,32,512]{1,2,0:T(8,128)(2,1)S(1)} %fusion.65), channel_id=1, source_target_pairs={{0,1},{1,2},{2,3},{3,4},{4,5},{5,6},{6,7},{7,8},{8,9},{9,10},{10,1... | collective-permute-start | bytes 196616 | tf_op jit(solution)/shard_map/while/body/eval_jaxpr/ppermute | solution.py:15
Sparse Core Ops, SparseCore 0:
  273.2 175.4 all-reduce.1
where the time goes:
time: 459 us; the launch traced here: 457 us
  waiting for transfers between devices  341 us (74%)
  starting transfers between devices  77.9 us (17%)
  matrix products  16.6 us (4%)
  between operations  14.8 us (3%)
  local copies, waits for them, and re-layouts  4.8 us (1%)
    psum x1, waiting for transfers between devices, body(): full = lax.psum(product * (-1.0 / modes), 'energy')  176 us
    ppermute x18, waiting for transfers between devices, with_halo(): lax.ppermute(lax.slice_in_dim(block, block.shape[dim] - width, None, axis...  128 us
    ppermute x18, starting transfers between devices, with_halo(): lax.ppermute(lax.slice_in_dim(block, block.shape[dim] - width, None, axis...  43.3 us
    ppermute x18, waiting for transfers between devices, with_halo(): lax.ppermute(lax.slice_in_dim(block, 0, width, axis=dim), axis, backward)  37.5 us
    ppermute x18, starting transfers between devices, with_halo(): lax.ppermute(lax.slice_in_dim(block, 0, width, axis=dim), axis, backward)  34.7 us
  transfers between devices with their start and end apart: 37, of which 37 were waited for; matrix products, arithmetic and copies ran while one was open for 1% of the time, Pallas kernels for 0%

commit v1 on v0

--- a/solution.py
+++ b/solution.py
@@ -89,7 +89,9 @@
     lam = lax.fori_loop(0, SWEEPS - 1, adjoint_sweep, lam)
     owned = block // lax.axis_size("energy")
     product = jnp.einsum("kim,kjm->ij", lam, psi, preferred_element_type=jnp.float32)
-    full = lax.psum(product * (-1.0 / modes), "energy")
+    own = product * (-1.0 / modes)
+    terms = lax.all_gather(own, "energy", axis=0, tiled=False)
+    full = terms.sum(axis=0)
     mine = lax.dynamic_slice_in_dim(full, lax.axis_index("energy") * owned, owned, 0)
     return mine.reshape(1, owned, block)
 

time: 459 us -> 388 us (0.85)
  the two profiles are of different devices: /device:TPU:64 before, /device:TPU:11 now
where the time goes in v1:
time: 388 us; the launch traced here: 384 us
  starting transfers between devices  158 us (41%)
  waiting for transfers between devices  147 us (38%)
  matrix products  55.4 us (14%)
  between operations  14.7 us (4%)
  local copies, waits for them, and re-layouts  4 us (1%)
  other arithmetic  3.94 us (1%)
    ppermute x18, starting transfers between devices, with_halo(): lax.ppermute(lax.slice_in_dim(block, 0, width, axis=dim), axis, backward)  119 us
    all_gather x1, waiting for transfers between devices, body(): terms = lax.all_gather(own, 'energy', axis=0, tiled=False)  86.8 us
    ppermute x18, waiting for transfers between devices, with_halo(): lax.ppermute(lax.slice_in_dim(block, block.shape[dim] - width, None, axis...  40.9 us
    ppermute x18, starting transfers between devices, with_halo(): lax.ppermute(lax.slice_in_dim(block, block.shape[dim] - width, None, axis...  39.4 us
    ppermute x18, waiting for transfers between devices, with_halo(): lax.ppermute(lax.slice_in_dim(block, 0, width, axis=dim), axis, backward)  18.9 us
    dot_general x9, matrix products, forward_sweep(): jnp.einsum('kij,kjm->kim', inverse_blocks, rhs, preferred_element_type=jn...  13.3 us
    dot_general x9, matrix products, adjoint_sweep(): jnp.einsum('kji,kjm->kim', inverse_blocks, update, preferred_element_type...  11.9 us
    dot_general x9, matrix products, adjoint_sweep(): jnp.einsum('ei,kim->kem', left_coupling, lam, preferred_element_type=jnp....  8.86 us
  transfers between devices with their start and end apart: 37, of which 28 were waited for; matrix products, arithmetic and copies ran while one was open for 5% of the time, Pallas kernels for 0%

profile of v1, /device:TPU:11, one launch (start us, length us, event | category | flops | bytes accessed | tf_op | source)
XLA Modules:
  0.0 383.9 jit_solution(14339001861566698999)
XLA Ops:
  11.5 129.7 %while.20 = (s32[]{:T(128)}, bf16[2,256,512]{1,2,0:T(8,128)(2,1)S(1)}, bf16[2,256,512]{1,2,0:T(8,128)(2,1)S(1)}, bf16[32,256]{1,0:T(8,128)(2,1)}, bf16[32,256]{1...) while((s32[]{:T(128)}, bf16[2,256,512]{1,2,0:T(8,128)(2,1)S(1)}, ...), condition=%wide.region_1.0_spmd, body=%wide.region_0.0_spmd.sunk | while | flops 169082880 | bytes 4358301 | solution.py:56
  11.6 2.6 collective-permute-start
  14.2 3.9 %collective-permute-start.1 = (bf16[2,32,512]{1,2,0:T(8,128)(2,1)S(1)}, bf16[2,32,512]{1,2,0:T(8,128)(2,1)S(1)}, u32[]{:S(2)}, u32[]{:S(2)}) collective-permute-start(bf16[2,32,512]{1,2,0:T(8,128)(2,1)S(1)} %get-tuple-element.174), channel_id=1, source_target_pairs={{0,1},{1,2},{2,3},{3,4},{4,5},{5,6},{6,7},{7,8},{8,9},{9,10},{10,1... | collective-permute-start | bytes 196616 | tf_op jit(solution)/shard_map/while/body/eval_jaxpr/ppermute | solution.py:15
  18.1 2.1 collective-permute-done
  23.0 2.4 collective-permute-start
  25.5 4.8 %collective-permute-start.1 = (bf16[2,32,512]{1,2,0:T(8,128)(2,1)S(1)}, bf16[2,32,512]{1,2,0:T(8,128)(2,1)S(1)}, u32[]{:S(2)}, u32[]{:S(2)}) collective-permute-start(bf16[2,32,512]{1,2,0:T(8,128)(2,1)S(1)} %get-tuple-element.174), channel_id=1, source_target_pairs={{0,1},{1,2},{2,3},{3,4},{4,5},{5,6},{6,7},{7,8},{8,9},{9,10},{10,1... | collective-permute-start | bytes 196616 | tf_op jit(solution)/shard_map/while/body/eval_jaxpr/ppermute | solution.py:15
  30.2 2.9 collective-permute-done
  34.1 1.6 collective-permute-done.1
  37.4 10.8 %collective-permute-start = (bf16[2,32,512]{1,2,0:T(8,128)(2,1)S(1)}, bf16[2,32,512]{1,2,0:T(8,128)(2,1)S(1)}, u32[]{:S(2)}, u32[]{:S(2)}) collective-permute-start(bf16[2,32,512]{1,2,0:T(8,128)(2,1)S(1)} %get-tuple-element.173), channel_id=1, source_target_pairs={{1,0},{2,1},{3,2},{4,3},{5,4},{6,5},{7,6},{8,7},{9,8},{10,9},{11,1... | collective-permute-start | bytes 196616 | tf_op jit(solution)/shard_map/while/body/eval_jaxpr/ppermute | solution.py:18
  48.2 1.9 collective-permute-start.1
  51.1 3.4 collective-permute-done.1
  54.5 1.5 fusion.57
  56.1 5.5 %collective-permute-start = (bf16[2,32,512]{1,2,0:T(8,128)(2,1)S(1)}, bf16[2,32,512]{1,2,0:T(8,128)(2,1)S(1)}, u32[]{:S(2)}, u32[]{:S(2)}) collective-permute-start(bf16[2,32,512]{1,2,0:T(8,128)(2,1)S(1)} %get-tuple-element.173), channel_id=1, source_target_pairs={{1,0},{2,1},{3,2},{4,3},{5,4},{6,5},{7,6},{8,7},{9,8},{10,9},{11,1... | collective-permute-start | bytes 196616 | tf_op jit(solution)/shard_map/while/body/eval_jaxpr/ppermute | solution.py:18
  61.6 1.9 collective-permute-start.1
  63.6 2.9 collective-permute-done
  69.6 5.6 %collective-permute-start = (bf16[2,32,512]{1,2,0:T(8,128)(2,1)S(1)}, bf16[2,32,512]{1,2,0:T(8,128)(2,1)S(1)}, u32[]{:S(2)}, u32[]{:S(2)}) collective-permute-start(bf16[2,32,512]{1,2,0:T(8,128)(2,1)S(1)} %get-tuple-element.173), channel_id=1, source_target_pairs={{1,0},{2,1},{3,2},{4,3},{5,4},{6,5},{7,6},{8,7},{9,8},{10,9},{11,1... | collective-permute-start | bytes 196616 | tf_op jit(solution)/shard_map/while/body/eval_jaxpr/ppermute | solution.py:18
  75.2 1.9 collective-permute-start.1
  77.1 2.8 collective-permute-done
  81.5 1.5 fusion.57
  83.1 5.6 %collective-permute-start = (bf16[2,32,512]{1,2,0:T(8,128)(2,1)S(1)}, bf16[2,32,512]{1,2,0:T(8,128)(2,1)S(1)}, u32[]{:S(2)}, u32[]{:S(2)}) collective-permute-start(bf16[2,32,512]{1,2,0:T(8,128)(2,1)S(1)} %get-tuple-element.173), channel_id=1, source_target_pairs={{1,0},{2,1},{3,2},{4,3},{5,4},{6,5},{7,6},{8,7},{9,8},{10,9},{11,1... | collective-permute-start | bytes 196616 | tf_op jit(solution)/shard_map/while/body/eval_jaxpr/ppermute | solution.py:18
  88.7 1.9 collective-permute-start.1
  90.7 2.8 collective-permute-done
  95.0 1.5 fusion.57
  96.7 6.2 %collective-permute-start = (bf16[2,32,512]{1,2,0:T(8,128)(2,1)S(1)}, bf16[2,32,512]{1,2,0:T(8,128)(2,1)S(1)}, u32[]{:S(2)}, u32[]{:S(2)}) collective-permute-start(bf16[2,32,512]{1,2,0:T(8,128)(2,1)S(1)} %get-tuple-element.173), channel_id=1, source_target_pairs={{1,0},{2,1},{3,2},{4,3},{5,4},{6,5},{7,6},{8,7},{9,8},{10,9},{11,1... | collective-permute-start | bytes 196616 | tf_op jit(solution)/shard_map/while/body/eval_jaxpr/ppermute | solution.py:18
  102.9 1.9 collective-permute-start.1
  104.8 2.2 collective-permute-done
  110.8 7.2 %collective-permute-start = (bf16[2,32,512]{1,2,0:T(8,128)(2,1)S(1)}, bf16[2,32,512]{1,2,0:T(8,128)(2,1)S(1)}, u32[]{:S(2)}, u32[]{:S(2)}) collective-permute-start(bf16[2,32,512]{1,2,0:T(8,128)(2,1)S(1)} %get-tuple-element.173), channel_id=1, source_target_pairs={{1,0},{2,1},{3,2},{4,3},{5,4},{6,5},{7,6},{8,7},{9,8},{10,9},{11,1... | collective-permute-start | bytes 196616 | tf_op jit(solution)/shard_map/while/body/eval_jaxpr/ppermute | solution.py:18
  118.0 1.9 collective-permute-start.1
  122.2 2.1 collective-permute-done.1
  124.3 1.5 fusion.57
  125.9 7.4 %collective-permute-start = (bf16[2,32,512]{1,2,0:T(8,128)(2,1)S(1)}, bf16[2,32,512]{1,2,0:T(8,128)(2,1)S(1)}, u32[]{:S(2)}, u32[]{:S(2)}) collective-permute-start(bf16[2,32,512]{1,2,0:T(8,128)(2,1)S(1)} %get-tuple-element.173), channel_id=1, source_target_pairs={{1,0},{2,1},{3,2},{4,3},{5,4},{6,5},{7,6},{8,7},{9,8},{10,9},{11,1... | collective-permute-start | bytes 196616 | tf_op jit(solution)/shard_map/while/body/eval_jaxpr/ppermute | solution.py:18
  133.4 1.9 collective-permute-start.1
  137.2 2.4 collective-permute-done.1
  139.7 1.5 fusion.57
  142.5 143.6 %while.21 = (s32[]{:T(128)}, bf16[2,256,512]{1,2,0:T(8,128)(2,1)S(1)}, bf16[32,256]{1,0:T(8,128)(2,1)}, bf16[32,256]{1,0:T(8,128)(2,1)}, f32[2,256,512]{1,2,0:T(...) while((s32[]{:T(128)}, bf16[2,256,512]{1,2,0:T(8,128)(2,1)S(1)}, ...), condition=%wide.region_3.0_spmd, body=%wide.region_2.0_spmd.sunk | while | flops 169213952 | bytes 4230837 | solution.py:89
  143.5 7.4 %collective-permute-start.2 = (bf16[2,32,512]{1,2,0:T(8,128)(2,1)S(1)}, bf16[2,32,512]{1,2,0:T(8,128)(2,1)S(1)}, u32[]{:S(2)}, u32[]{:S(2)}) collective-permute-start(bf16[2,32,512]{1,2,0:T(8,128)(2,1)S(1)} %fusion.64), channel_id=1, source_target_pairs={{1,0},{2,1},{3,2},{4,3},{5,4},{6,5},{7,6},{8,7},{9,8},{10,9},{11,1... | collective-permute-start | bytes 196616 | tf_op jit(solution)/shard_map/while/body/eval_jaxpr/ppermute | solution.py:18
  152.0 1.9 collective-permute-start.3
  154.0 3.3 collective-permute-done.3
  159.6 5.5 %collective-permute-start.2 = (bf16[2,32,512]{1,2,0:T(8,128)(2,1)S(1)}, bf16[2,32,512]{1,2,0:T(8,128)(2,1)S(1)}, u32[]{:S(2)}, u32[]{:S(2)}) collective-permute-start(bf16[2,32,512]{1,2,0:T(8,128)(2,1)S(1)} %fusion.64), channel_id=1, source_target_pairs={{1,0},{2,1},{3,2},{4,3},{5,4},{6,5},{7,6},{8,7},{9,8},{10,9},{11,1... | collective-permute-start | bytes 196616 | tf_op jit(solution)/shard_map/while/body/eval_jaxpr/ppermute | solution.py:18
  166.1 1.9 collective-permute-start.3
  169.0 2.4 collective-permute-done.3
  173.8 6.9 %collective-permute-start.2 = (bf16[2,32,512]{1,2,0:T(8,128)(2,1)S(1)}, bf16[2,32,512]{1,2,0:T(8,128)(2,1)S(1)}, u32[]{:S(2)}, u32[]{:S(2)}) collective-permute-start(bf16[2,32,512]{1,2,0:T(8,128)(2,1)S(1)} %fusion.64), channel_id=1, source_target_pairs={{1,0},{2,1},{3,2},{4,3},{5,4},{6,5},{7,6},{8,7},{9,8},{10,9},{11,1... | collective-permute-start | bytes 196616 | tf_op jit(solution)/shard_map/while/body/eval_jaxpr/ppermute | solution.py:18
  181.7 1.9 collective-permute-start.3
  183.7 3.3 collective-permute-done.3
  189.3 7.6 %collective-permute-start.2 = (bf16[2,32,512]{1,2,0:T(8,128)(2,1)S(1)}, bf16[2,32,512]{1,2,0:T(8,128)(2,1)S(1)}, u32[]{:S(2)}, u32[]{:S(2)}) collective-permute-start(bf16[2,32,512]{1,2,0:T(8,128)(2,1)S(1)} %fusion.64), channel_id=1, source_target_pairs={{1,0},{2,1},{3,2},{4,3},{5,4},{6,5},{7,6},{8,7},{9,8},{10,9},{11,1... | collective-permute-start | bytes 196616 | tf_op jit(solution)/shard_map/while/body/eval_jaxpr/ppermute | solution.py:18
  198.0 1.9 collective-permute-start.3
  200.0 3.3 collective-permute-done.3
  205.6 7.6 %collective-permute-start.2 = (bf16[2,32,512]{1,2,0:T(8,128)(2,1)S(1)}, bf16[2,32,512]{1,2,0:T(8,128)(2,1)S(1)}, u32[]{:S(2)}, u32[]{:S(2)}) collective-permute-start(bf16[2,32,512]{1,2,0:T(8,128)(2,1)S(1)} %fusion.64), channel_id=1, source_target_pairs={{1,0},{2,1},{3,2},{4,3},{5,4},{6,5},{7,6},{8,7},{9,8},{10,9},{11,1... | collective-permute-start | bytes 196616 | tf_op jit(solution)/shard_map/while/body/eval_jaxpr/ppermute | solution.py:18
  214.2 1.9 collective-permute-start.3
  216.3 3.3 collective-permute-done.3
  221.9 7.6 %collective-permute-start.2 = (bf16[2,32,512]{1,2,0:T(8,128)(2,1)S(1)}, bf16[2,32,512]{1,2,0:T(8,128)(2,1)S(1)}, u32[]{:S(2)}, u32[]{:S(2)}) collective-permute-start(bf16[2,32,512]{1,2,0:T(8,128)(2,1)S(1)} %fusion.64), channel_id=1, source_target_pairs={{1,0},{2,1},{3,2},{4,3},{5,4},{6,5},{7,6},{8,7},{9,8},{10,9},{11,1... | collective-permute-start | bytes 196616 | tf_op jit(solution)/shard_map/while/body/eval_jaxpr/ppermute | solution.py:18
  230.6 1.9 collective-permute-start.3
  232.6 3.3 collective-permute-done.3
  238.2 7.6 %collective-permute-start.2 = (bf16[2,32,512]{1,2,0:T(8,128)(2,1)S(1)}, bf16[2,32,512]{1,2,0:T(8,128)(2,1)S(1)}, u32[]{:S(2)}, u32[]{:S(2)}) collective-permute-start(bf16[2,32,512]{1,2,0:T(8,128)(2,1)S(1)} %fusion.64), channel_id=1, source_target_pairs={{1,0},{2,1},{3,2},{4,3},{5,4},{6,5},{7,6},{8,7},{9,8},{10,9},{11,1... | collective-permute-start | bytes 196616 | tf_op jit(solution)/shard_map/while/body/eval_jaxpr/ppermute | solution.py:18
  246.8 1.9 collective-permute-start.3
  248.9 3.2 collective-permute-done.3
  254.5 7.6 %collective-permute-start.2 = (bf16[2,32,512]{1,2,0:T(8,128)(2,1)S(1)}, bf16[2,32,512]{1,2,0:T(8,128)(2,1)S(1)}, u32[]{:S(2)}, u32[]{:S(2)}) collective-permute-start(bf16[2,32,512]{1,2,0:T(8,128)(2,1)S(1)} %fusion.64), channel_id=1, source_target_pairs={{1,0},{2,1},{3,2},{4,3},{5,4},{6,5},{7,6},{8,7},{9,8},{10,9},{11,1... | collective-permute-start | bytes 196616 | tf_op jit(solution)/shard_map/while/body/eval_jaxpr/ppermute | solution.py:18
  263.1 1.9 collective-permute-start.3
  265.2 3.2 collective-permute-done.3
  270.8 7.6 %collective-permute-start.2 = (bf16[2,32,512]{1,2,0:T(8,128)(2,1)S(1)}, bf16[2,32,512]{1,2,0:T(8,128)(2,1)S(1)}, u32[]{:S(2)}, u32[]{:S(2)}) collective-permute-start(bf16[2,32,512]{1,2,0:T(8,128)(2,1)S(1)} %fusion.64), channel_id=1, source_target_pairs={{1,0},{2,1},{3,2},{4,3},{5,4},{6,5},{7,6},{8,7},{9,8},{10,9},{11,1... | collective-permute-start | bytes 196616 | tf_op jit(solution)/shard_map/while/body/eval_jaxpr/ppermute | solution.py:18
  279.4 1.9 collective-permute-start.3
  281.5 3.3 collective-permute-done.3
  287.2 86.8 %all-gather.3.cloned.1.call-done = f32[4096,256]{1,0:T(8,128)} async-done(((f32[256,256]{1,0:T(8,128)}), f32[4096,256]{1,0:T(8,128)}) %all-gather.3.cloned.1.call-update) | async-done | bytes 4194320 | tf_op jit(solution)/shard_map/all_gather | solution.py:93
  374.0 2.5 reduce_sum.9
  (114 shorter events, 59.5 us)
Async XLA Ops:
  6.5 367.5 %all-gather.3.cloned.1.call-start = ((), (), s32[]{:S(2)}) async-start(), calls=%async_computation | async-start | bytes 4456448 | tf_op jit(solution)/shard_map/all_gather | solution.py:93
  11.6 8.6 %collective-permute-start = (bf16[2,32,512]{1,2,0:T(8,128)(2,1)S(1)}, bf16[2,32,512]{1,2,0:T(8,128)(2,1)S(1)}, u32[]{:S(2)}, u32[]{:S(2)}) collective-permute-start(bf16[2,32,512]{1,2,0:T(8,128)(2,1)S(1)} %get-tuple-element.173), channel_id=1, source_target_pairs={{1,0},{2,1},{3,2},{4,3},{5,4},{6,5},{7,6},{8,7},{9,8},{10,9},{11,1... | collective-permute-start | bytes 196616 | tf_op jit(solution)/shard_map/while/body/eval_jaxpr/ppermute | solution.py:18
  14.2 7.2 %collective-permute-start.1 = (bf16[2,32,512]{1,2,0:T(8,128)(2,1)S(1)}, bf16[2,32,512]{1,2,0:T(8,128)(2,1)S(1)}, u32[]{:S(2)}, u32[]{:S(2)}) collective-permute-start(bf16[2,32,512]{1,2,0:T(8,128)(2,1)S(1)} %get-tuple-element.174), channel_id=1, source_target_pairs={{0,1},{1,2},{2,3},{3,4},{4,5},{5,6},{6,7},{7,8},{8,9},{9,10},{10,1... | collective-permute-start | bytes 196616 | tf_op jit(solution)/shard_map/while/body/eval_jaxpr/ppermute | solution.py:15
  23.0 10.1 %collective-permute-start = (bf16[2,32,512]{1,2,0:T(8,128)(2,1)S(1)}, bf16[2,32,512]{1,2,0:T(8,128)(2,1)S(1)}, u32[]{:S(2)}, u32[]{:S(2)}) collective-permute-start(bf16[2,32,512]{1,2,0:T(8,128)(2,1)S(1)} %get-tuple-element.173), channel_id=1, source_target_pairs={{1,0},{2,1},{3,2},{4,3},{5,4},{6,5},{7,6},{8,7},{9,8},{10,9},{11,1... | collective-permute-start | bytes 196616 | tf_op jit(solution)/shard_map/while/body/eval_jaxpr/ppermute | solution.py:18
  25.5 10.3 %collective-permute-start.1 = (bf16[2,32,512]{1,2,0:T(8,128)(2,1)S(1)}, bf16[2,32,512]{1,2,0:T(8,128)(2,1)S(1)}, u32[]{:S(2)}, u32[]{:S(2)}) collective-permute-start(bf16[2,32,512]{1,2,0:T(8,128)(2,1)S(1)} %get-tuple-element.174), channel_id=1, source_target_pairs={{0,1},{1,2},{2,3},{3,4},{4,5},{5,6},{6,7},{7,8},{8,9},{9,10},{10,1... | collective-permute-start | bytes 196616 | tf_op jit(solution)/shard_map/while/body/eval_jaxpr/ppermute | solution.py:15
  37.4 12.8 %collective-permute-start = (bf16[2,32,512]{1,2,0:T(8,128)(2,1)S(1)}, bf16[2,32,512]{1,2,0:T(8,128)(2,1)S(1)}, u32[]{:S(2)}, u32[]{:S(2)}) collective-permute-start(bf16[2,32,512]{1,2,0:T(8,128)(2,1)S(1)} %get-tuple-element.173), channel_id=1, source_target_pairs={{1,0},{2,1},{3,2},{4,3},{5,4},{6,5},{7,6},{8,7},{9,8},{10,9},{11,1... | collective-permute-start | bytes 196616 | tf_op jit(solution)/shard_map/while/body/eval_jaxpr/ppermute | solution.py:18
  48.2 6.3 %collective-permute-start.1 = (bf16[2,32,512]{1,2,0:T(8,128)(2,1)S(1)}, bf16[2,32,512]{1,2,0:T(8,128)(2,1)S(1)}, u32[]{:S(2)}, u32[]{:S(2)}) collective-permute-start(bf16[2,32,512]{1,2,0:T(8,128)(2,1)S(1)} %get-tuple-element.174), channel_id=1, source_target_pairs={{0,1},{1,2},{2,3},{3,4},{4,5},{5,6},{6,7},{7,8},{8,9},{9,10},{10,1... | collective-permute-start | bytes 196616 | tf_op jit(solution)/shard_map/while/body/eval_jaxpr/ppermute | solution.py:15
  56.1 10.3 %collective-permute-start = (bf16[2,32,512]{1,2,0:T(8,128)(2,1)S(1)}, bf16[2,32,512]{1,2,0:T(8,128)(2,1)S(1)}, u32[]{:S(2)}, u32[]{:S(2)}) collective-permute-start(bf16[2,32,512]{1,2,0:T(8,128)(2,1)S(1)} %get-tuple-element.173), channel_id=1, source_target_pairs={{1,0},{2,1},{3,2},{4,3},{5,4},{6,5},{7,6},{8,7},{9,8},{10,9},{11,1... | collective-permute-start | bytes 196616 | tf_op jit(solution)/shard_map/while/body/eval_jaxpr/ppermute | solution.py:18
  61.6 6.3 %collective-permute-start.1 = (bf16[2,32,512]{1,2,0:T(8,128)(2,1)S(1)}, bf16[2,32,512]{1,2,0:T(8,128)(2,1)S(1)}, u32[]{:S(2)}, u32[]{:S(2)}) collective-permute-start(bf16[2,32,512]{1,2,0:T(8,128)(2,1)S(1)} %get-tuple-element.174), channel_id=1, source_target_pairs={{0,1},{1,2},{2,3},{3,4},{4,5},{5,6},{6,7},{7,8},{8,9},{9,10},{10,1... | collective-permute-start | bytes 196616 | tf_op jit(solution)/shard_map/while/body/eval_jaxpr/ppermute | solution.py:15
  69.6 10.3 %collective-permute-start = (bf16[2,32,512]{1,2,0:T(8,128)(2,1)S(1)}, bf16[2,32,512]{1,2,0:T(8,128)(2,1)S(1)}, u32[]{:S(2)}, u32[]{:S(2)}) collective-permute-start(bf16[2,32,512]{1,2,0:T(8,128)(2,1)S(1)} %get-tuple-element.173), channel_id=1, source_target_pairs={{1,0},{2,1},{3,2},{4,3},{5,4},{6,5},{7,6},{8,7},{9,8},{10,9},{11,1... | collective-permute-start | bytes 196616 | tf_op jit(solution)/shard_map/while/body/eval_jaxpr/ppermute | solution.py:18
  75.2 6.3 %collective-permute-start.1 = (bf16[2,32,512]{1,2,0:T(8,128)(2,1)S(1)}, bf16[2,32,512]{1,2,0:T(8,128)(2,1)S(1)}, u32[]{:S(2)}, u32[]{:S(2)}) collective-permute-start(bf16[2,32,512]{1,2,0:T(8,128)(2,1)S(1)} %get-tuple-element.174), channel_id=1, source_target_pairs={{0,1},{1,2},{2,3},{3,4},{4,5},{5,6},{6,7},{7,8},{8,9},{9,10},{10,1... | collective-permute-start | bytes 196616 | tf_op jit(solution)/shard_map/while/body/eval_jaxpr/ppermute | solution.py:15
  83.1 10.3 %collective-permute-start = (bf16[2,32,512]{1,2,0:T(8,128)(2,1)S(1)}, bf16[2,32,512]{1,2,0:T(8,128)(2,1)S(1)}, u32[]{:S(2)}, u32[]{:S(2)}) collective-permute-start(bf16[2,32,512]{1,2,0:T(8,128)(2,1)S(1)} %get-tuple-element.173), channel_id=1, source_target_pairs={{1,0},{2,1},{3,2},{4,3},{5,4},{6,5},{7,6},{8,7},{9,8},{10,9},{11,1... | collective-permute-start | bytes 196616 | tf_op jit(solution)/shard_map/while/body/eval_jaxpr/ppermute | solution.py:18
  88.7 6.3 %collective-permute-start.1 = (bf16[2,32,512]{1,2,0:T(8,128)(2,1)S(1)}, bf16[2,32,512]{1,2,0:T(8,128)(2,1)S(1)}, u32[]{:S(2)}, u32[]{:S(2)}) collective-permute-start(bf16[2,32,512]{1,2,0:T(8,128)(2,1)S(1)} %get-tuple-element.174), channel_id=1, source_target_pairs={{0,1},{1,2},{2,3},{3,4},{4,5},{5,6},{6,7},{7,8},{8,9},{9,10},{10,1... | collective-permute-start | bytes 196616 | tf_op jit(solution)/shard_map/while/body/eval_jaxpr/ppermute | solution.py:15
  96.7 10.3 %collective-permute-start = (bf16[2,32,512]{1,2,0:T(8,128)(2,1)S(1)}, bf16[2,32,512]{1,2,0:T(8,128)(2,1)S(1)}, u32[]{:S(2)}, u32[]{:S(2)}) collective-permute-start(bf16[2,32,512]{1,2,0:T(8,128)(2,1)S(1)} %get-tuple-element.173), channel_id=1, source_target_pairs={{1,0},{2,1},{3,2},{4,3},{5,4},{6,5},{7,6},{8,7},{9,8},{10,9},{11,1... | collective-permute-start | bytes 196616 | tf_op jit(solution)/shard_map/while/body/eval_jaxpr/ppermute | solution.py:18
  102.9 6.3 %collective-permute-start.1 = (bf16[2,32,512]{1,2,0:T(8,128)(2,1)S(1)}, bf16[2,32,512]{1,2,0:T(8,128)(2,1)S(1)}, u32[]{:S(2)}, u32[]{:S(2)}) collective-permute-start(bf16[2,32,512]{1,2,0:T(8,128)(2,1)S(1)} %get-tuple-element.174), channel_id=1, source_target_pairs={{0,1},{1,2},{2,3},{3,4},{4,5},{5,6},{6,7},{7,8},{8,9},{9,10},{10,1... | collective-permute-start | bytes 196616 | tf_op jit(solution)/shard_map/while/body/eval_jaxpr/ppermute | solution.py:15
  110.8 10.3 %collective-permute-start = (bf16[2,32,512]{1,2,0:T(8,128)(2,1)S(1)}, bf16[2,32,512]{1,2,0:T(8,128)(2,1)S(1)}, u32[]{:S(2)}, u32[]{:S(2)}) collective-permute-start(bf16[2,32,512]{1,2,0:T(8,128)(2,1)S(1)} %get-tuple-element.173), channel_id=1, source_target_pairs={{1,0},{2,1},{3,2},{4,3},{5,4},{6,5},{7,6},{8,7},{9,8},{10,9},{11,1... | collective-permute-start | bytes 196616 | tf_op jit(solution)/shard_map/while/body/eval_jaxpr/ppermute | solution.py:18
  118.0 6.3 %collective-permute-start.1 = (bf16[2,32,512]{1,2,0:T(8,128)(2,1)S(1)}, bf16[2,32,512]{1,2,0:T(8,128)(2,1)S(1)}, u32[]{:S(2)}, u32[]{:S(2)}) collective-permute-start(bf16[2,32,512]{1,2,0:T(8,128)(2,1)S(1)} %get-tuple-element.174), channel_id=1, source_target_pairs={{0,1},{1,2},{2,3},{3,4},{4,5},{5,6},{6,7},{7,8},{8,9},{9,10},{10,1... | collective-permute-start | bytes 196616 | tf_op jit(solution)/shard_map/while/body/eval_jaxpr/ppermute | solution.py:15
  125.9 10.3 %collective-permute-start = (bf16[2,32,512]{1,2,0:T(8,128)(2,1)S(1)}, bf16[2,32,512]{1,2,0:T(8,128)(2,1)S(1)}, u32[]{:S(2)}, u32[]{:S(2)}) collective-permute-start(bf16[2,32,512]{1,2,0:T(8,128)(2,1)S(1)} %get-tuple-element.173), channel_id=1, source_target_pairs={{1,0},{2,1},{3,2},{4,3},{5,4},{6,5},{7,6},{8,7},{9,8},{10,9},{11,1... | collective-permute-start | bytes 196616 | tf_op jit(solution)/shard_map/while/body/eval_jaxpr/ppermute | solution.py:18
  133.4 6.3 %collective-permute-start.1 = (bf16[2,32,512]{1,2,0:T(8,128)(2,1)S(1)}, bf16[2,32,512]{1,2,0:T(8,128)(2,1)S(1)}, u32[]{:S(2)}, u32[]{:S(2)}) collective-permute-start(bf16[2,32,512]{1,2,0:T(8,128)(2,1)S(1)} %get-tuple-element.174), channel_id=1, source_target_pairs={{0,1},{1,2},{2,3},{3,4},{4,5},{5,6},{6,7},{7,8},{8,9},{9,10},{10,1... | collective-permute-start | bytes 196616 | tf_op jit(solution)/shard_map/while/body/eval_jaxpr/ppermute | solution.py:15
  143.5 10.5 %collective-permute-start.2 = (bf16[2,32,512]{1,2,0:T(8,128)(2,1)S(1)}, bf16[2,32,512]{1,2,0:T(8,128)(2,1)S(1)}, u32[]{:S(2)}, u32[]{:S(2)}) collective-permute-start(bf16[2,32,512]{1,2,0:T(8,128)(2,1)S(1)} %fusion.64), channel_id=1, source_target_pairs={{1,0},{2,1},{3,2},{4,3},{5,4},{6,5},{7,6},{8,7},{9,8},{10,9},{11,1... | collective-permute-start | bytes 196616 | tf_op jit(solution)/shard_map/while/body/eval_jaxpr/ppermute | solution.py:18
  152.0 5.3 %collective-permute-start.3 = (bf16[2,32,512]{1,2,0:T(8,128)(2,1)S(1)}, bf16[2,32,512]{1,2,0:T(8,128)(2,1)S(1)}, u32[]{:S(2)}, u32[]{:S(2)}) collective-permute-start(bf16[2,32,512]{1,2,0:T(8,128)(2,1)S(1)} %fusion.65), channel_id=1, source_target_pairs={{0,1},{1,2},{2,3},{3,4},{4,5},{5,6},{6,7},{7,8},{8,9},{9,10},{10,1... | collective-permute-start | bytes 196616 | tf_op jit(solution)/shard_map/while/body/eval_jaxpr/ppermute | solution.py:15
  159.6 9.4 %collective-permute-start.2 = (bf16[2,32,512]{1,2,0:T(8,128)(2,1)S(1)}, bf16[2,32,512]{1,2,0:T(8,128)(2,1)S(1)}, u32[]{:S(2)}, u32[]{:S(2)}) collective-permute-start(bf16[2,32,512]{1,2,0:T(8,128)(2,1)S(1)} %fusion.64), channel_id=1, source_target_pairs={{1,0},{2,1},{3,2},{4,3},{5,4},{6,5},{7,6},{8,7},{9,8},{10,9},{11,1... | collective-permute-start | bytes 196616 | tf_op jit(solution)/shard_map/while/body/eval_jaxpr/ppermute | solution.py:18
  166.1 5.3 %collective-permute-start.3 = (bf16[2,32,512]{1,2,0:T(8,128)(2,1)S(1)}, bf16[2,32,512]{1,2,0:T(8,128)(2,1)S(1)}, u32[]{:S(2)}, u32[]{:S(2)}) collective-permute-start(bf16[2,32,512]{1,2,0:T(8,128)(2,1)S(1)} %fusion.65), channel_id=1, source_target_pairs={{0,1},{1,2},{2,3},{3,4},{4,5},{5,6},{6,7},{7,8},{8,9},{9,10},{10,1... | collective-permute-start | bytes 196616 | tf_op jit(solution)/shard_map/while/body/eval_jaxpr/ppermute | solution.py:15
  173.8 9.9 %collective-permute-start.2 = (bf16[2,32,512]{1,2,0:T(8,128)(2,1)S(1)}, bf16[2,32,512]{1,2,0:T(8,128)(2,1)S(1)}, u32[]{:S(2)}, u32[]{:S(2)}) collective-permute-start(bf16[2,32,512]{1,2,0:T(8,128)(2,1)S(1)} %fusion.64), channel_id=1, source_target_pairs={{1,0},{2,1},{3,2},{4,3},{5,4},{6,5},{7,6},{8,7},{9,8},{10,9},{11,1... | collective-permute-start | bytes 196616 | tf_op jit(solution)/shard_map/while/body/eval_jaxpr/ppermute | solution.py:18
  181.7 5.3 %collective-permute-start.3 = (bf16[2,32,512]{1,2,0:T(8,128)(2,1)S(1)}, bf16[2,32,512]{1,2,0:T(8,128)(2,1)S(1)}, u32[]{:S(2)}, u32[]{:S(2)}) collective-permute-start(bf16[2,32,512]{1,2,0:T(8,128)(2,1)S(1)} %fusion.65), channel_id=1, source_target_pairs={{0,1},{1,2},{2,3},{3,4},{4,5},{5,6},{6,7},{7,8},{8,9},{9,10},{10,1... | collective-permute-start | bytes 196616 | tf_op jit(solution)/shard_map/while/body/eval_jaxpr/ppermute | solution.py:15
  189.3 10.6 %collective-permute-start.2 = (bf16[2,32,512]{1,2,0:T(8,128)(2,1)S(1)}, bf16[2,32,512]{1,2,0:T(8,128)(2,1)S(1)}, u32[]{:S(2)}, u32[]{:S(2)}) collective-permute-start(bf16[2,32,512]{1,2,0:T(8,128)(2,1)S(1)} %fusion.64), channel_id=1, source_target_pairs={{1,0},{2,1},{3,2},{4,3},{5,4},{6,5},{7,6},{8,7},{9,8},{10,9},{11,1... | collective-permute-start | bytes 196616 | tf_op jit(solution)/shard_map/while/body/eval_jaxpr/ppermute | solution.py:18
  198.0 5.3 %collective-permute-start.3 = (bf16[2,32,512]{1,2,0:T(8,128)(2,1)S(1)}, bf16[2,32,512]{1,2,0:T(8,128)(2,1)S(1)}, u32[]{:S(2)}, u32[]{:S(2)}) collective-permute-start(bf16[2,32,512]{1,2,0:T(8,128)(2,1)S(1)} %fusion.65), channel_id=1, source_target_pairs={{0,1},{1,2},{2,3},{3,4},{4,5},{5,6},{6,7},{7,8},{8,9},{9,10},{10,1... | collective-permute-start | bytes 196616 | tf_op jit(solution)/shard_map/while/body/eval_jaxpr/ppermute | solution.py:15
  205.6 10.6 %collective-permute-start.2 = (bf16[2,32,512]{1,2,0:T(8,128)(2,1)S(1)}, bf16[2,32,512]{1,2,0:T(8,128)(2,1)S(1)}, u32[]{:S(2)}, u32[]{:S(2)}) collective-permute-start(bf16[2,32,512]{1,2,0:T(8,128)(2,1)S(1)} %fusion.64), channel_id=1, source_target_pairs={{1,0},{2,1},{3,2},{4,3},{5,4},{6,5},{7,6},{8,7},{9,8},{10,9},{11,1... | collective-permute-start | bytes 196616 | tf_op jit(solution)/shard_map/while/body/eval_jaxpr/ppermute | solution.py:18
  214.2 5.3 %collective-permute-start.3 = (bf16[2,32,512]{1,2,0:T(8,128)(2,1)S(1)}, bf16[2,32,512]{1,2,0:T(8,128)(2,1)S(1)}, u32[]{:S(2)}, u32[]{:S(2)}) collective-permute-start(bf16[2,32,512]{1,2,0:T(8,128)(2,1)S(1)} %fusion.65), channel_id=1, source_target_pairs={{0,1},{1,2},{2,3},{3,4},{4,5},{5,6},{6,7},{7,8},{8,9},{9,10},{10,1... | collective-permute-start | bytes 196616 | tf_op jit(solution)/shard_map/while/body/eval_jaxpr/ppermute | solution.py:15
  221.9 10.6 %collective-permute-start.2 = (bf16[2,32,512]{1,2,0:T(8,128)(2,1)S(1)}, bf16[2,32,512]{1,2,0:T(8,128)(2,1)S(1)}, u32[]{:S(2)}, u32[]{:S(2)}) collective-permute-start(bf16[2,32,512]{1,2,0:T(8,128)(2,1)S(1)} %fusion.64), channel_id=1, source_target_pairs={{1,0},{2,1},{3,2},{4,3},{5,4},{6,5},{7,6},{8,7},{9,8},{10,9},{11,1... | collective-permute-start | bytes 196616 | tf_op jit(solution)/shard_map/while/body/eval_jaxpr/ppermute | solution.py:18
  230.6 5.3 %collective-permute-start.3 = (bf16[2,32,512]{1,2,0:T(8,128)(2,1)S(1)}, bf16[2,32,512]{1,2,0:T(8,128)(2,1)S(1)}, u32[]{:S(2)}, u32[]{:S(2)}) collective-permute-start(bf16[2,32,512]{1,2,0:T(8,128)(2,1)S(1)} %fusion.65), channel_id=1, source_target_pairs={{0,1},{1,2},{2,3},{3,4},{4,5},{5,6},{6,7},{7,8},{8,9},{9,10},{10,1... | collective-permute-start | bytes 196616 | tf_op jit(solution)/shard_map/while/body/eval_jaxpr/ppermute | solution.py:15
  238.2 10.6 %collective-permute-start.2 = (bf16[2,32,512]{1,2,0:T(8,128)(2,1)S(1)}, bf16[2,32,512]{1,2,0:T(8,128)(2,1)S(1)}, u32[]{:S(2)}, u32[]{:S(2)}) collective-permute-start(bf16[2,32,512]{1,2,0:T(8,128)(2,1)S(1)} %fusion.64), channel_id=1, source_target_pairs={{1,0},{2,1},{3,2},{4,3},{5,4},{6,5},{7,6},{8,7},{9,8},{10,9},{11,1... | collective-permute-start | bytes 196616 | tf_op jit(solution)/shard_map/while/body/eval_jaxpr/ppermute | solution.py:18
  246.8 5.3 %collective-permute-start.3 = (bf16[2,32,512]{1,2,0:T(8,128)(2,1)S(1)}, bf16[2,32,512]{1,2,0:T(8,128)(2,1)S(1)}, u32[]{:S(2)}, u32[]{:S(2)}) collective-permute-start(bf16[2,32,512]{1,2,0:T(8,128)(2,1)S(1)} %fusion.65), channel_id=1, source_target_pairs={{0,1},{1,2},{2,3},{3,4},{4,5},{5,6},{6,7},{7,8},{8,9},{9,10},{10,1... | collective-permute-start | bytes 196616 | tf_op jit(solution)/shard_map/while/body/eval_jaxpr/ppermute | solution.py:15
  254.5 10.6 %collective-permute-start.2 = (bf16[2,32,512]{1,2,0:T(8,128)(2,1)S(1)}, bf16[2,32,512]{1,2,0:T(8,128)(2,1)S(1)}, u32[]{:S(2)}, u32[]{:S(2)}) collective-permute-start(bf16[2,32,512]{1,2,0:T(8,128)(2,1)S(1)} %fusion.64), channel_id=1, source_target_pairs={{1,0},{2,1},{3,2},{4,3},{5,4},{6,5},{7,6},{8,7},{9,8},{10,9},{11,1... | collective-permute-start | bytes 196616 | tf_op jit(solution)/shard_map/while/body/eval_jaxpr/ppermute | solution.py:18
  263.1 5.3 %collective-permute-start.3 = (bf16[2,32,512]{1,2,0:T(8,128)(2,1)S(1)}, bf16[2,32,512]{1,2,0:T(8,128)(2,1)S(1)}, u32[]{:S(2)}, u32[]{:S(2)}) collective-permute-start(bf16[2,32,512]{1,2,0:T(8,128)(2,1)S(1)} %fusion.65), channel_id=1, source_target_pairs={{0,1},{1,2},{2,3},{3,4},{4,5},{5,6},{6,7},{7,8},{8,9},{9,10},{10,1... | collective-permute-start | bytes 196616 | tf_op jit(solution)/shard_map/while/body/eval_jaxpr/ppermute | solution.py:15
  270.8 10.6 %collective-permute-start.2 = (bf16[2,32,512]{1,2,0:T(8,128)(2,1)S(1)}, bf16[2,32,512]{1,2,0:T(8,128)(2,1)S(1)}, u32[]{:S(2)}, u32[]{:S(2)}) collective-permute-start(bf16[2,32,512]{1,2,0:T(8,128)(2,1)S(1)} %fusion.64), channel_id=1, source_target_pairs={{1,0},{2,1},{3,2},{4,3},{5,4},{6,5},{7,6},{8,7},{9,8},{10,9},{11,1... | collective-permute-start | bytes 196616 | tf_op jit(solution)/shard_map/while/body/eval_jaxpr/ppermute | solution.py:18
  279.4 5.3 %collective-permute-start.3 = (bf16[2,32,512]{1,2,0:T(8,128)(2,1)S(1)}, bf16[2,32,512]{1,2,0:T(8,128)(2,1)S(1)}, u32[]{:S(2)}, u32[]{:S(2)}) collective-permute-start(bf16[2,32,512]{1,2,0:T(8,128)(2,1)S(1)} %fusion.65), channel_id=1, source_target_pairs={{0,1},{1,2},{2,3},{3,4},{4,5},{5,6},{6,7},{7,8},{8,9},{9,10},{10,1... | collective-permute-start | bytes 196616 | tf_op jit(solution)/shard_map/while/body/eval_jaxpr/ppermute | solution.py:15
Sparse Core Ops, SparseCore 0:
  287.3 86.6 all-gather.2
